TPU v7x, 512 devices: a whole 4x8x8 slice. The times are simulated.
512 devices in a mesh: wide: 16 (over y, core), narrow: 32 (over z, x).
Axes of the slice: x: 4, y: 8, z: 8, core: 2. Of those that a mesh axis runs over, the one named last changes fastest.
Arguments:
- embeddings: bfloat16 [12288, 1024], P(('wide', 'narrow')), may hold values from -6 to 6
- cluster: int32 [512], replicated, may hold values from 0 to 44, never falling along the last dimension, each value on 1 to 34 neighbouring positions
Outputs:
- shifted: float32 [12288, 1024], P(('wide', 'narrow'))
Inputs may be any that keep to these rules, and one draw needn't show every extreme that they name: The blocks of one cluster are consecutive (ids never fall); each cluster holds 1 to 34 blocks, one exactly 34.
All inputs are finite; a program needn't handle non-finite values.
Results may differ from a plain program's by a relative error of at most 0.029.
Values may be sent and summed in bfloat16 or wider, within the bound.
A program may use at most 64 MiB of HBM per device.

v0:
```python
import math
import jax
import jax.numpy as jnp
from jax import lax
from jax.sharding import PartitionSpec as P

D = 1024
REACH = 2
SPREAD = 0.5


def from_behind(block, axis, distance):
    devices = range(lax.axis_size(axis))
    route = [(i - distance, i) for i in devices if i - distance in devices]
    return lax.ppermute(block, axis, route)


def normalize(rows):
    values = rows.astype(jnp.float32)
    factor = lax.rsqrt(jnp.mean(values * values, axis=1, keepdims=True) + 1e-06)
    return (values * factor).astype(jnp.bfloat16)


def tile_weights(group, keys, row_clusters, key_cluster, self_start):
    scores = lax.dot_general(
        group, keys, (((1,), (1,)), ((), ())), preferred_element_type=jnp.float32
    )
    weights = jnp.exp(scores * (1.0 / (SPREAD * math.sqrt(D))))
    keep = row_clusters[:, None] == key_cluster
    if self_start is not None:
        query_rows = lax.broadcasted_iota(jnp.int32, scores.shape, 0)
        key_rows = lax.broadcasted_iota(jnp.int32, scores.shape, 1) + self_start
        keep = keep & (query_rows != key_rows)
    return jnp.where(keep, weights, jnp.float32(0.0))


def on_device(embeddings, cluster):
    blk = embeddings.shape[0]
    n_narrow = lax.axis_size("narrow")
    n_wide = lax.axis_size("wide")
    wide_at = lax.axis_index("wide")
    narrow_at = lax.axis_index("narrow")
    normed = normalize(embeddings)
    group = lax.all_gather(normed, "narrow", axis=0, tiled=True)
    rows_all = group.shape[0]
    first_block = wide_at * n_narrow
    group_clusters = lax.dynamic_slice_in_dim(cluster, first_block, n_narrow)
    row_clusters = jnp.broadcast_to(group_clusters[:, None], (n_narrow, blk)).reshape(rows_all)
    own_block = first_block + narrow_at

    def block_cluster(offset):
        target = wide_at + offset
        inside = (target >= 0) & (target < n_wide)
        position = jnp.clip(own_block + offset * n_narrow, 0, cluster.shape[0] - 1)
        found = lax.dynamic_index_in_dim(cluster, position, 0, keepdims=False)
        return jnp.where(inside, found, -1)

    def forward(keys, key_cluster, self_start):
        weights = tile_weights(group, keys, row_clusters, key_cluster, self_start)
        added = jnp.dot(weights.astype(jnp.bfloat16), keys, preferred_element_type=jnp.float32)
        return (added, jnp.sum(weights, axis=1))

    numerator, total = forward(normed, block_cluster(0), narrow_at * blk)
    for offset in range(-REACH, REACH + 1):
        if offset != 0:
            keys = from_behind(normed, "wide", -offset)
            added, summed = forward(keys, block_cluster(offset), None)
            numerator = numerator + added
            total = total + summed
    own_numerator, own_total = (
        lax.psum_scatter(
            numerator.astype(jnp.bfloat16), "narrow", scatter_dimension=0, tiled=True
        ).astype(jnp.float32),
        lax.psum_scatter(
            total.astype(jnp.bfloat16), "narrow", scatter_dimension=0, tiled=True
        ).astype(jnp.float32),
    )
    return own_numerator / own_total[:, None]


def solution(mesh):
    in_specs = (P(("wide", "narrow"), None), P())
    out_specs = P(("wide", "narrow"), None)
    return jax.shard_map(
        on_device, mesh=mesh, in_specs=in_specs, out_specs=out_specs, check_vma=False
    )
```

profile of v0, /device:TPU:8, one launch (start us, length us, event | category | flops | bytes accessed | tf_op | source)
XLA Modules:
  0.0 334.4 jit_solution(4841747790055246149)
XLA Ops:
  6.5 0.9 fusion.10
  7.5 1.5 fusion.11
  9.0 7.7 %collective-permute-start.3 = (bf16[24,1024]{1,0:T(8,128)(2,1)}, bf16[24,1024]{1,0:T(8,128)(2,1)S(1)}, u32[]{:S(2)}, u32[]{:S(2)}) collective-permute-start(bf16[24,1024]{1,0:T(8,128)(2,1)} %fusion.11), channel_id=1, source_target_pairs={{64,0},{96,32},{128,64},{160,96},{192,128},{224,160},{256,192},{28... | collective-permute-start | bytes 147464 | tf_op jit(solution)/shard_map/ppermute | solution.py:15
  16.8 1.9 collective-permute-start.2
  18.7 2.4 collective-permute-start.1
  21.1 1.9 collective-permute-start
  23.1 1.5 fusion.25
  27.7 0.8 broadcast_compare_fusion
  29.3 69.2 %all-gather.2.cloned.1.call-done = bf16[768,1024]{1,0:T(8,128)(2,1)} async-done(((bf16[24,1024]{1,0:T(8,128)(2,1)}), bf16[768,1024]{1,0:T(8,128)(2,1)}) %all-gather.2.cloned.1.call-update) | async-done | bytes 1572880 | tf_op jit(solution)/shard_map/all_gather | solution.py:44
  98.6 2.0 fusion.29
  100.6 0.6 fusion.23
  101.2 0.8 copy-done
  102.0 0.5 fusion.30
  102.5 0.6 fusion.21
  103.1 0.5 fusion.28
  103.7 0.6 fusion.19
  104.3 0.5 fusion.27
  104.8 0.6 fusion.17
  105.4 0.5 fusion.26
  106.0 1.9 add_convert_fusion
  107.9 1.3 dynamic-slice
  109.9 72.2 %all-reduce = bf16[768]{0:T(1024)(128)(2,1)S(1)} all-reduce(bf16[768]{0:T(1024)(128)(2,1)S(1)} %add_convert_fusion.1), channel_id=3, replica_groups=mesh['wide'=16,'narrow'=32] {'narrow'}, use_global_device_ids=true, to_apply=%region_7.8.clone | all-reduce | flops 768 | bytes 3072
  182.1 143.9 %reduce-scatter.2.cloned.1.call-done = bf16[24,1024]{1,0:T(8,128)(2,1)} async-done(((bf16[768,1024]{1,0:T(8,128)(2,1)}), bf16[24,1024]{1,0:T(8,128)(2,1)}) %reduce-scatter.2.cloned.1.call-update) | async-done | bytes 49168 | tf_op jit(solution)/shard_map/reduce_scatter | solution.py:71
  326.0 1.5 convert_divide_fusion
  (26 shorter events, 1.1 us)
Async XLA Ops:
  6.5 92.0 %all-gather.2.cloned.1.call-start = ((), (), s32[]{:S(2)}) async-start(), calls=%async_computation.1 | async-start | bytes 1622016 | tf_op jit(solution)/shard_map/all_gather | solution.py:44
  9.0 91.6 %copy-start.1 = (bf16[24,1024]{1,0:T(8,128)(2,1)S(1)}, bf16[24,1024]{1,0:T(8,128)(2,1)}, u32[]{:S(2)}) copy-start(bf16[24,1024]{1,0:T(8,128)(2,1)} %fusion.11) | copy-start | bytes 147460
  9.0 317.1 %reduce-scatter.2.cloned.1.call-start = ((), (), s32[]{:S(2)}) async-start(), calls=%async_computation.2 | async-start | bytes 1622016 | tf_op jit(solution)/shard_map/reduce_scatter | solution.py:71
  9.0 96.4 %collective-permute-start.3 = (bf16[24,1024]{1,0:T(8,128)(2,1)}, bf16[24,1024]{1,0:T(8,128)(2,1)S(1)}, u32[]{:S(2)}, u32[]{:S(2)}) collective-permute-start(bf16[24,1024]{1,0:T(8,128)(2,1)} %fusion.11), channel_id=1, source_target_pairs={{64,0},{96,32},{128,64},{160,96},{192,128},{224,160},{256,192},{28... | collective-permute-start | bytes 147464 | tf_op jit(solution)/shard_map/ppermute | solution.py:15
  16.8 87.5 %collective-permute-start.2 = (bf16[24,1024]{1,0:T(8,128)(2,1)}, bf16[24,1024]{1,0:T(8,128)(2,1)S(1)}, u32[]{:S(2)}, u32[]{:S(2)}) collective-permute-start(bf16[24,1024]{1,0:T(8,128)(2,1)} %fusion.11), channel_id=1, source_target_pairs={{32,0},{64,32},{96,64},{128,96},{160,128},{192,160},{224,192},{256... | collective-permute-start | bytes 147464 | tf_op jit(solution)/shard_map/ppermute | solution.py:15
  18.7 84.4 %collective-permute-start.1 = (bf16[24,1024]{1,0:T(8,128)(2,1)}, bf16[24,1024]{1,0:T(8,128)(2,1)S(1)}, u32[]{:S(2)}, u32[]{:S(2)}) collective-permute-start(bf16[24,1024]{1,0:T(8,128)(2,1)} %fusion.11), channel_id=1, source_target_pairs={{0,32},{32,64},{64,96},{96,128},{128,160},{160,192},{192,224},{224... | collective-permute-start | bytes 147464 | tf_op jit(solution)/shard_map/ppermute | solution.py:15
  21.1 80.0 %collective-permute-start = (bf16[24,1024]{1,0:T(8,128)(2,1)}, bf16[24,1024]{1,0:T(8,128)(2,1)S(1)}, u32[]{:S(2)}, u32[]{:S(2)}) collective-permute-start(bf16[24,1024]{1,0:T(8,128)(2,1)} %fusion.11), channel_id=1, source_target_pairs={{0,64},{32,96},{64,128},{96,160},{128,192},{160,224},{192,256},{22... | collective-permute-start | bytes 147464 | tf_op jit(solution)/shard_map/ppermute | solution.py:15
  100.6 1.4 copy-start
Sparse Core Ops, SparseCore 0:
  10.5 88.0 all-gather.1
  108.1 217.9 reduce-scatter.1
where the time goes:
time: 335 us; the launch traced here: 334 us
  waiting for transfers between devices  213 us (64%)
  blocking collectives  72.2 us (22%)
  between operations  17.3 us (5%)
  starting transfers between devices  14 us (4%)
  matrix products  8.42 us (3%)
  other arithmetic  4.81 us (1%)
  local copies, waits for them, and re-layouts  4.48 us (1%)
    reduce_scatter x1, waiting for transfers between devices, on_device(): lax.psum_scatter(numerator.astype(jnp.bfloat16), 'narrow', scatter_dimens...  144 us
    unnamed x1, blocking collectives  72.2 us
    all_gather x1, waiting for transfers between devices, on_device(): group = lax.all_gather(normed, 'narrow', axis=0, tiled=True)  69.2 us
    ppermute x4, starting transfers between devices, from_behind(): return lax.ppermute(block, axis, route)  14 us
  transfers between devices with their start and end apart: 6, of which 2 were waited for; matrix products, arithmetic and copies ran while one was open for 3% of the time, Pallas kernels for 0%

commit v1 on v0

--- a/solution.py
+++ b/solution.py
@@ -41,7 +41,15 @@
     wide_at = lax.axis_index("wide")
     narrow_at = lax.axis_index("narrow")
     normed = normalize(embeddings)
-    group = lax.all_gather(normed, "narrow", axis=0, tiled=True)
+    group = jnp.concatenate(
+        lax.all_to_all(
+            jnp.stack(lax.axis_size("narrow") * [normed], axis=0),
+            axis_name="narrow",
+            split_axis=0,
+            concat_axis=0,
+        ),
+        axis=0,
+    )
     rows_all = group.shape[0]
     first_block = wide_at * n_narrow
     group_clusters = lax.dynamic_slice_in_dim(cluster, first_block, n_narrow)

time: 335 us -> 297 us (0.89)
  waiting for transfers between devices: 213 us -> 169 us
  starting transfers between devices: 14 us -> 23.5 us
    all_gather x1 -> x0, waiting for transfers between devices: 69.2 us -> none  [on_device(): group = lax.all_gather(normed, 'narrow', axis=0, tiled=True)]
    all_to_all x0 -> x1, waiting for transfers between devices: none -> 24 us  [on_device(): lax.all_to_all(jnp.stack(lax.axis_size('narrow') * [normed], axis=0), axi...]
    all_to_all x0 -> x1, starting transfers between devices: none -> 13.3 us  [on_device(): lax.all_to_all(jnp.stack(lax.axis_size('narrow') * [normed], axis=0), axi...]
    ppermute x4, starting transfers between devices: 14 us -> 10.2 us  [from_behind(): return lax.ppermute(block, axis, route)]
where the time goes in v1:
time: 297 us; the launch traced here: 296 us
  waiting for transfers between devices  169 us (57%)
  blocking collectives  71.1 us (24%)
  starting transfers between devices  23.5 us (8%)
  between operations  17.4 us (6%)
  matrix products  7.01 us (2%)
  local copies, waits for them, and re-layouts  4.18 us (1%)
  other arithmetic  3.51 us (1%)
    reduce_scatter x1, waiting for transfers between devices, on_device(): lax.psum_scatter(numerator.astype(jnp.bfloat16), 'narrow', scatter_dimens...  145 us
    unnamed x1, blocking collectives  71.1 us
    all_to_all x1, waiting for transfers between devices, on_device(): lax.all_to_all(jnp.stack(lax.axis_size('narrow') * [normed], axis=0), axi...  24 us
    all_to_all x1, starting transfers between devices, on_device(): lax.all_to_all(jnp.stack(lax.axis_size('narrow') * [normed], axis=0), axi...  13.3 us
    ppermute x4, starting transfers between devices, from_behind(): return lax.ppermute(block, axis, route)  10.2 us
  transfers between devices with their start and end apart: 6, of which 2 were waited for; matrix products, arithmetic and copies ran while one was open for 3% of the time, Pallas kernels for 0%

profile of v1, /device:TPU:8, one launch (start us, length us, event | category | flops | bytes accessed | tf_op | source)
XLA Modules:
  0.0 296.2 jit_solution(9174819178088892717)
XLA Ops:
  6.5 0.9 fusion.10
  7.5 0.9 fusion.11
  8.3 1.3 stack.2
  9.7 13.3 %all-to-all-start = ((bf16[32,24,1024]{2,1,0:T(8,128)(2,1)}), bf16[32,24,1024]{2,1,0:T(8,128)(2,1)S(1)}, u32[]{:S(2)}, u32[]{:S(2)}) async-start(bf16[32,24,1024]{2,1,0:T(8,128)(2,1)} %stack.2), calls=%async_computation | async-start | bytes 3145728 | tf_op jit(solution)/shard_map/all_to_all | solution.py:45
  23.1 2.4 collective-permute-start.3
  25.4 1.9 collective-permute-start.2
  27.3 2.4 collective-permute-start.1
  29.8 3.5 %collective-permute-start = (bf16[24,1024]{1,0:T(8,128)(2,1)S(1)}, bf16[24,1024]{1,0:T(8,128)(2,1)S(1)}, u32[]{:S(2)}, u32[]{:S(2)}) collective-permute-start(bf16[24,1024]{1,0:T(8,128)(2,1)S(1)} %fusion.11), channel_id=1, source_target_pairs={{0,64},{32,96},{64,128},{96,160},{128,192},{160,224},{192,256},{22... | collective-permute-start | bytes 147464 | tf_op jit(solution)/shard_map/ppermute | solution.py:15
  33.3 0.7 fusion.25
  38.1 24.0 %all-to-all-done = bf16[32,24,1024]{2,1,0:T(8,128)(2,1)S(1)} async-done(((bf16[32,24,1024]{2,1,0:T(8,128)(2,1)}), bf16[32,24,1024]{2,1,0:T(8,128)(2,1)S(1)}, u32[]{:S(2)}, u32[]{:S(2)}) %all-to-all-start) | async-done | bytes 1572896 | tf_op jit(solution)/shard_map/all_to_all | solution.py:45
  62.1 0.5 fusion.29
  62.7 0.6 fusion.23
  63.3 0.5 fusion.28
  63.8 0.6 fusion.19
  64.4 0.5 fusion.30
  65.0 0.6 fusion.21
  65.6 0.5 fusion.27
  66.1 0.6 fusion.17
  66.7 0.5 fusion.26
  67.3 1.9 add_convert_fusion
  69.2 1.3 dynamic-slice
  71.2 71.1 %all-reduce = bf16[768]{0:T(1024)(128)(2,1)S(1)} all-reduce(bf16[768]{0:T(1024)(128)(2,1)S(1)} %add_convert_fusion.1), channel_id=3, replica_groups=mesh['wide'=16,'narrow'=32] {'narrow'}, use_global_device_ids=true, to_apply=%region_7.8.clone | all-reduce | flops 768 | bytes 3072
  142.4 145.4 %reduce-scatter.2.cloned.1.call-done = bf16[24,1024]{1,0:T(8,128)(2,1)} async-done(((bf16[768,1024]{1,0:T(8,128)(2,1)}), bf16[24,1024]{1,0:T(8,128)(2,1)}) %reduce-scatter.2.cloned.1.call-update) | async-done | bytes 49168 | tf_op jit(solution)/shard_map/reduce_scatter | solution.py:79
  287.8 1.5 convert_divide_fusion
  (24 shorter events, 1.1 us)
Async XLA Ops:
  9.7 23.6 %copy-start = (s32[512]{0:T(512)S(1)}, s32[512]{0:T(512)}, u32[]{:S(2)}) copy-start(s32[512]{0:T(512)} %param.3) | copy-start | bytes 6148
  9.7 52.4 %all-to-all-start = ((bf16[32,24,1024]{2,1,0:T(8,128)(2,1)}), bf16[32,24,1024]{2,1,0:T(8,128)(2,1)S(1)}, u32[]{:S(2)}, u32[]{:S(2)}) async-start(bf16[32,24,1024]{2,1,0:T(8,128)(2,1)} %stack.2), calls=%async_computation | async-start | bytes 3145728 | tf_op jit(solution)/shard_map/all_to_all | solution.py:45
  23.0 264.8 %reduce-scatter.2.cloned.1.call-start = ((), (), s32[]{:S(2)}) async-start(), calls=%async_computation.2 | async-start | bytes 1622016 | tf_op jit(solution)/shard_map/reduce_scatter | solution.py:79
  23.1 43.7 %collective-permute-start.3 = (bf16[24,1024]{1,0:T(8,128)(2,1)S(1)}, bf16[24,1024]{1,0:T(8,128)(2,1)S(1)}, u32[]{:S(2)}, u32[]{:S(2)}) collective-permute-start(bf16[24,1024]{1,0:T(8,128)(2,1)S(1)} %fusion.11), channel_id=1, source_target_pairs={{64,0},{96,32},{128,64},{160,96},{192,128},{224,160},{256,192},{28... | collective-permute-start | bytes 147464 | tf_op jit(solution)/shard_map/ppermute | solution.py:15
  25.4 40.2 %collective-permute-start.2 = (bf16[24,1024]{1,0:T(8,128)(2,1)S(1)}, bf16[24,1024]{1,0:T(8,128)(2,1)S(1)}, u32[]{:S(2)}, u32[]{:S(2)}) collective-permute-start(bf16[24,1024]{1,0:T(8,128)(2,1)S(1)} %fusion.11), channel_id=1, source_target_pairs={{32,0},{64,32},{96,64},{128,96},{160,128},{192,160},{224,192},{256... | collective-permute-start | bytes 147464 | tf_op jit(solution)/shard_map/ppermute | solution.py:15
  27.3 35.9 %collective-permute-start.1 = (bf16[24,1024]{1,0:T(8,128)(2,1)S(1)}, bf16[24,1024]{1,0:T(8,128)(2,1)S(1)}, u32[]{:S(2)}, u32[]{:S(2)}) collective-permute-start(bf16[24,1024]{1,0:T(8,128)(2,1)S(1)} %fusion.11), channel_id=1, source_target_pairs={{0,32},{32,64},{64,96},{96,128},{128,160},{160,192},{192,224},{224... | collective-permute-start | bytes 147464 | tf_op jit(solution)/shard_map/ppermute | solution.py:15
  29.8 34.7 %collective-permute-start = (bf16[24,1024]{1,0:T(8,128)(2,1)S(1)}, bf16[24,1024]{1,0:T(8,128)(2,1)S(1)}, u32[]{:S(2)}, u32[]{:S(2)}) collective-permute-start(bf16[24,1024]{1,0:T(8,128)(2,1)S(1)} %fusion.11), channel_id=1, source_target_pairs={{0,64},{32,96},{64,128},{96,160},{128,192},{160,224},{192,256},{22... | collective-permute-start | bytes 147464 | tf_op jit(solution)/shard_map/ppermute | solution.py:15
Sparse Core Ops, SparseCore 0:
  69.3 218.4 reduce-scatter.1
